TPU v7x, 512 devices: a whole 4x4x16 slice. The times are simulated.
512 devices in a mesh: row: 32 (over z_lo, x, core), col: 16 (over y, z_hi).
Axes of the slice: x: 4, y: 4, z: 16 (z_hi: 4, z_lo: 4; z = z_hi * 4 + z_lo), core: 2. Of those that a mesh axis runs over, the one named last changes fastest.
Arguments:
- acts: bfloat16 [2048, 16384], P('row', 'col'), may hold values from -6 to 6
- grads: float32 [16384, 512], P('col', 'row'), may hold values from -24 to 24
Outputs:
- factor: float32 [16384, 16384], P('row', 'col')
- applied: float32 [16384, 512], P('row', 'col')
- solution: float32 [16384, 512], P('col', 'row')
All inputs are finite; a program needn't handle non-finite values.
Results may differ from a plain program's by a relative error of at most 0.0003.
Values may be sent and summed in bfloat16 or wider, within the bound.
A program may use at most 64 MiB of HBM per device.

v0:
```python
import math
import jax
import jax.numpy as jnp
from jax import lax
from jax.sharding import Mesh
from jax.sharding import PartitionSpec as P

ROW = ("row_0", "row_1", "row_2")
damping = 1.0
highest = lax.Precision.HIGHEST


def in_order(pieces, dim):
    dims = list(pieces.shape[1:])
    dims[dim] *= pieces.shape[0]
    return jnp.moveaxis(pieces, 0, dim).reshape(dims)


def all_blocks(shard, axes, turns):
    pieces = shard[None]
    for k in turns:
        pieces = lax.all_gather(pieces, axes[k], axis=0, tiled=True)
    block = [lax.axis_size(axes[k]) for k in reversed(turns)]
    pieces = pieces.reshape(*block, *shard.shape)
    turned = sorted(range(len(turns)), key=lambda place: turns[len(turns) - 1 - place])
    return pieces.transpose(*turned, *range(len(turns), pieces.ndim)).reshape(-1, *shard.shape)


def gather_axes(shard, axes, turns, dim):
    return in_order(all_blocks(shard, axes, turns), dim)


def padded_to(lines, peers):
    spare = -lines.shape[0] % peers
    if not spare:
        return lines
    return jnp.concatenate([lines, jnp.zeros((spare, *lines.shape[1:]), lines.dtype)])


def from_root(shard, axis, root):
    lines = jnp.where(lax.axis_index(axis) == root, shard, jnp.zeros_like(shard)).reshape(
        -1, *shard.shape[1:][-1:]
    )
    padded = padded_to(lines, lax.axis_size(axis))
    own = lax.psum_scatter(padded, axis, scatter_dimension=0, tiled=True)
    return lax.all_gather(own, axis, axis=0, tiled=True)[: len(lines)].reshape(shard.shape)


def from_everyone(shard, axis):
    peers = lax.axis_size(axis)
    return lax.all_to_all(
        jnp.broadcast_to(shard[None], (peers, *shard.shape)), axis, 0, 0, tiled=True
    )


def gather_directly(shard, axis, dim):
    pieces = from_everyone(shard, axis)
    return in_order(pieces, dim)


def split_up(shard, dim, peers):
    before, after = (shard.shape[:dim], shard.shape[dim + 1 :])
    return jnp.moveaxis(shard.reshape(*before, peers, -1, *after), dim, 0)


def summed_on_arrival(shard, axis, dim):
    pieces = split_up(shard, dim, lax.axis_size(axis))
    arrived = lax.all_to_all(pieces, axis, split_axis=0, concat_axis=0, tiled=True)
    return arrived.sum(axis=0)


def step_size(feature_count, token_count):
    return 1.0 / (damping + (1.0 + math.sqrt(feature_count / token_count)) ** 2)


def local(acts, grads):
    row_count = lax.axis_size(ROW)
    col_count = lax.axis_size("col")
    row_ratio = row_count // col_count
    row_index = lax.axis_index(ROW)
    col_index = lax.axis_index("col")
    outer_width = acts.shape[1]
    inner_width = outer_width // row_ratio
    token_count = acts.shape[0] * row_count
    omega_step = step_size(outer_width * col_count, token_count)
    row_offset = row_index % row_ratio * inner_width
    owner_col = row_index // row_ratio
    column_panel = gather_axes(acts, ROW, (0, 1, 2), 0)
    owned_slice = lax.dynamic_slice_in_dim(column_panel, row_offset, inner_width, 1)
    inner_panel = from_root(owned_slice, "col", owner_col)
    gram_sum = lax.dot_general(
        inner_panel, column_panel, (((0,), (0,)), ((), ())), preferred_element_type=jnp.float32
    )
    gram_tile = gram_sum / token_count
    is_owner = (col_index == owner_col).astype(jnp.float32)
    gathered = gather_directly(grads, ROW, 1)
    mirror_rows = lax.dynamic_slice_in_dim(gathered, row_offset, inner_width, 0)
    partial_sum = jnp.dot(gram_tile, gathered, precision=highest) + damping * is_owner * mirror_rows
    applied = summed_on_arrival(partial_sum, "col", 1)
    full_applied = gather_directly(applied, "col", 1)
    mirror_coef = omega_step**3 * damping - 3.0 * omega_step**2
    empty_block = jnp.zeros((outer_width, full_applied.shape[1]), jnp.float32)
    placed = lax.dynamic_update_slice_in_dim(
        empty_block, full_applied * (mirror_coef * is_owner), row_offset, 0
    )
    second_sum = (
        omega_step**3
        * lax.dot_general(
            gram_tile,
            full_applied,
            (((0,), (0,)), ((), ())),
            precision=highest,
            preferred_element_type=jnp.float32,
        )
        + placed
    )
    solution = 3.0 * omega_step * grads + summed_on_arrival(second_sum, ROW, 1)
    return (gram_tile, applied, solution)


def solution(mesh):
    split = Mesh(
        mesh.devices.reshape(4, 4, 2, mesh.shape["col"]), ("row_0", "row_1", "row_2", "col")
    )
    in_specs = (P(ROW, "col"), P("col", ROW))
    out_specs = (P(ROW, "col"), P(ROW, "col"), P("col", ROW))
    return jax.shard_map(local, mesh=split, in_specs=in_specs, out_specs=out_specs, check_vma=False)
```

profile of v0, /device:TPU:1, one launch (start us, length us, event | category | flops | bytes accessed | tf_op | source)
XLA Modules:
  0.0 521.1 jit_solution(1728708824256396200)
XLA Ops:
  7.2 0.0 all-gather.5.cloned.1.call-start
  7.2 17.8 %all-gather = bf16[256,1024]{1,0:T(8,128)(2,1)} all-gather(bf16[64,1024]{1,0:T(8,128)(2,1)} %param.2), channel_id=2, replica_groups=mesh['row_0'=4,'row_1'=4,'row_2'=2,'col'=16] {'row_0'}, dimensions={0}, use_global_device_ids=true | all-gather | bytes 655360 | tf_op jit(solution)/shard_map/all_gather | solution.py:22
  25.0 0.0 all-gather.5.cloned.1.call-update
  25.1 0.0 all-gather.7.cloned.1.call-start
  25.1 42.3 %all-gather.5.cloned.1.call-done = bf16[16,64,1024]{2,1,0:T(8,128)(2,1)} async-done(((bf16[4,64,1024]{2,1,0:T(8,128)(2,1)}), bf16[16,64,1024]{2,1,0:T(8,128)(2,1)}) %all-gather.5.cloned.1.call-update) | async-done | bytes 2097168 | tf_op jit(solution)/shard_map/all_gather | solution.py:22
  67.4 0.0 all-gather.7.cloned.1.call-update
  67.5 0.0 reduce-scatter.2.cloned.1.call-start
  67.6 27.7 %all-gather.7.cloned.1.call-done = bf16[32,64,1024]{2,1,0:T(8,128)(2,1)} async-done(((bf16[16,64,1024]{2,1,0:T(8,128)(2,1)}), bf16[32,64,1024]{2,1,0:T(8,128)(2,1)}) %all-gather.7.cloned.1.call-update) | async-done | bytes 4194320 | tf_op jit(solution)/shard_map/all_gather | solution.py:22
  95.3 2.6 copy.6
  97.9 0.0 copy-start
  97.9 1.9 copy-done
  99.9 1.9 dynamic-slice_select_fusion
  101.7 0.0 copy-start.2
  101.7 0.0 reduce-scatter.2.cloned.1.call-update
  101.8 0.8 copy-done.2
  102.6 1.6 broadcast_in_dim.10
  104.2 6.7 %all-to-all-start = ((f32[32,1024,16]{1,2,0:T(8,128)}), f32[32,1024,16]{1,2,0:T(8,128)}, u32[]{:S(2)}, u32[]{:S(2)}) async-start(f32[32,1024,16]{1,2,0:T(8,128)} %broadcast_in_dim.10), calls=%async_computation.1 | async-start | bytes 4194304 | tf_op jit(solution)/shard_map/all_to_all | solution.py:51
  110.9 0.0 all-gather.9.cloned.1.call-start
  110.9 127.9 %reduce-scatter.2.cloned.1.call-done = bf16[128,512]{1,0:T(8,128)(2,1)} async-done(((bf16[2048,512]{1,0:T(8,128)(2,1)}), bf16[128,512]{1,0:T(8,128)(2,1)}) %reduce-scatter.2.cloned.1.call-update) | async-done | bytes 131088 | tf_op jit(solution)/shard_map/reduce_scatter | solution.py:45
  238.8 0.0 all-gather.9.cloned.1.call-update
  238.8 92.5 %all-gather.9.cloned.1.call-done = bf16[2048,512]{1,0:T(8,128)(2,1)} async-done(((bf16[128,512]{1,0:T(8,128)(2,1)}), bf16[2048,512]{1,0:T(8,128)(2,1)}) %all-gather.9.cloned.1.call-update) | async-done | bytes 2097168 | tf_op jit(solution)/shard_map/all_gather | solution.py:46
  331.3 5.2 convolution_multiply_fusion
  336.5 0.0 copy-start.1
  336.5 0.0 all-to-all-done
  336.5 6.2 %convolution_add_fusion = f32[512,512]{0,1:T(8,128)S(1)} fusion(f32[512,1024]{1,0:T(8,128)S(1)} %convolution_multiply_fusion, f32[1024,512]{0,1:T(8,128)} %bitcast.5, s32[]{:T(128)S(6)} %select_n.27, f32[]{:T(128)S(6)} %convert_element_type.3), kind=kOutput, calls=%fused_computation.3 | convolution fusion | flops 3221749760 | bytes 6291464 | tf_op jit(solution)/shard_map/dot_general | solution.py:98
  342.7 60.1 %all_to_all.20 = f32[16,512,32]{1,2,0:T(8,128)S(1)} all-to-all(f32[16,512,32]{1,2,0:T(8,128)S(1)} %bitcast.29), channel_id=1, replica_groups=mesh['row_0'=4,'row_1'=4,'row_2'=2,'col'=16] {'col'}, dimensions={0} | all-to-all | bytes 2097152 | tf_op jit(solution)/shard_map/all_to_all | solution.py:68
  402.8 0.1 reduce_sum.18
  402.9 0.0 copy-start.3
  402.9 1.1 broadcast_in_dim.22
  404.0 5.4 %all-to-all-start.2 = ((f32[16,512,32]{1,2,0:T(8,128)}), f32[16,512,32]{1,2,0:T(8,128)S(1)}, u32[]{:S(2)}, u32[]{:S(2)}) async-start(f32[16,512,32]{1,2,0:T(8,128)} %broadcast_in_dim.22), calls=%async_computation.3 | async-start | bytes 2097152 | tf_op jit(solution)/shard_map/all_to_all | solution.py:51
  409.4 46.9 %all-to-all-done.2 = f32[16,512,32]{1,2,0:T(8,128)S(1)} async-done(((f32[16,512,32]{1,2,0:T(8,128)}), f32[16,512,32]{1,2,0:T(8,128)S(1)}, u32[]{:S(2)}, u32[]{:S(2)}) %all-to-all-start.2) | async-done | bytes 1048608 | tf_op jit(solution)/shard_map/all_to_all | solution.py:51
  456.2 0.0 copy-done.1
  456.2 3.5 convolution_multiply_fusion.1
  459.8 0.0 copy-done.3
  459.8 0.3 add_dynamic-update-slice_fusion
  460.1 53.7 %all_to_all.21 = f32[32,1024,16]{1,2,0:T(8,128)S(1)} all-to-all(f32[32,1024,16]{1,2,0:T(8,128)S(1)} %bitcast.23), channel_id=1, replica_groups=mesh['row_0'=4,'row_1'=4,'row_2'=2,'col'=16] {'row_0','row_1','row_2'}, dimensions={0} | all-to-all | bytes 4194304 | tf_op jit(solution)/shard_map/all_to_all | solution.py:68
  513.8 0.1 reduce_sum.19
  513.9 0.6 multiply_add_fusion
Async XLA Ops:
  7.2 60.3 %all-gather.5.cloned.1.call-start = ((), (), s32[]{:S(2)}) async-start(), calls=%async_computation.5 | async-start | bytes 2621440 | tf_op jit(solution)/shard_map/all_gather | solution.py:22
  25.1 70.2 %all-gather.7.cloned.1.call-start = ((), (), s32[]{:S(2)}) async-start(), calls=%async_computation.6 | async-start | bytes 6291456 | tf_op jit(solution)/shard_map/all_gather | solution.py:22
  67.5 171.3 %reduce-scatter.2.cloned.1.call-start = ((), (), s32[]{:S(2)}) async-start(), calls=%async_computation.7 | async-start | bytes 2228224 | tf_op jit(solution)/shard_map/reduce_scatter | solution.py:45
  97.9 2.0 copy-start
  101.7 0.8 copy-start.2
  104.2 232.3 %all-to-all-start = ((f32[32,1024,16]{1,2,0:T(8,128)}), f32[32,1024,16]{1,2,0:T(8,128)}, u32[]{:S(2)}, u32[]{:S(2)}) async-start(f32[32,1024,16]{1,2,0:T(8,128)} %broadcast_in_dim.10), calls=%async_computation.1 | async-start | bytes 4194304 | tf_op jit(solution)/shard_map/all_to_all | solution.py:51
  110.9 220.4 %all-gather.9.cloned.1.call-start = ((), (), s32[]{:S(2)}) async-start(), calls=%async_computation.8 | async-start | bytes 2228224 | tf_op jit(solution)/shard_map/all_gather | solution.py:46
  336.5 119.8 %copy-start.1 = (f32[512,1024]{1,0:T(8,128)}, f32[512,1024]{1,0:T(8,128)S(1)}, u32[]{:S(2)}) copy-start(f32[512,1024]{1,0:T(8,128)S(1)} %convolution_multiply_fusion) | copy-start | bytes 6291460
  402.9 56.9 %copy-start.3 = (f32[512,32]{0,1:T(8,128)}, f32[512,32]{0,1:T(8,128)S(1)}, u32[]{:S(2)}) copy-start(f32[512,32]{0,1:T(8,128)S(1)} %reduce_sum.18) | copy-start | bytes 196612
  404.0 52.3 %all-to-all-start.2 = ((f32[16,512,32]{1,2,0:T(8,128)}), f32[16,512,32]{1,2,0:T(8,128)S(1)}, u32[]{:S(2)}, u32[]{:S(2)}) async-start(f32[16,512,32]{1,2,0:T(8,128)} %broadcast_in_dim.22), calls=%async_computation.3 | async-start | bytes 2097152 | tf_op jit(solution)/shard_map/all_to_all | solution.py:51
Sparse Core Ops, SparseCore 0:
  25.2 42.2 all-gather.4
  69.5 25.6 all-gather.6
  101.9 136.8 reduce-scatter.1
  242.1 89.1 all-gather.8
where the time goes:
time: 522 us; the launch traced here: 521 us
  waiting for transfers between devices  337 us (65%)
  blocking collectives  132 us (25%)
  matrix products  14.9 us (3%)
  between operations  13.9 us (3%)
  starting transfers between devices  12.2 us (2%)
  local copies, waits for them, and re-layouts  8.1 us (2%)
    reduce_scatter x1, waiting for transfers between devices, from_root(): own = lax.psum_scatter(padded, axis, scatter_dimension=0, tiled=True)  128 us
    all_to_all x2, blocking collectives, summed_on_arrival(): lax.all_to_all(pieces, axis, split_axis=0, concat_axis=0, tiled=True)  114 us
    all_gather x1, waiting for transfers between devices, from_root(): lax.all_gather(own, axis, axis=0, tiled=True)[:len(lines)]  92.5 us
    all_gather x2, waiting for transfers between devices, all_blocks(): pieces = lax.all_gather(pieces, axes[k], axis=0, tiled=True)  70 us
    all_to_all x2, waiting for transfers between devices, from_everyone(): lax.all_to_all(jnp.broadcast_to(shard[None], (peers, *shard.shape)), axis...  46.9 us
    all_gather x1, blocking collectives, all_blocks(): pieces = lax.all_gather(pieces, axes[k], axis=0, tiled=True)  17.8 us
    all_to_all x2, starting transfers between devices, from_everyone(): lax.all_to_all(jnp.broadcast_to(shard[None], (peers, *shard.shape)), axis...  12.1 us
  transfers between devices with their start and end apart: 6, of which 5 were waited for; matrix products, arithmetic and copies ran while one was open for 1% of the time, Pallas kernels for 0%

commit v1 on v0

--- a/solution.py
+++ b/solution.py
@@ -43,7 +43,9 @@
     )
     padded = padded_to(lines, lax.axis_size(axis))
     own = lax.psum_scatter(padded, axis, scatter_dimension=0, tiled=True)
-    return lax.all_gather(own, axis, axis=0, tiled=True)[: len(lines)].reshape(shard.shape)
+    return jnp.concatenate(
+        lax.all_to_all(jnp.stack([own] * lax.axis_size(axis)), axis, 0, 0), axis=0
+    )[: len(lines)].reshape(shard.shape)
 
 
 def from_everyone(shard, axis):

time: 522 us -> 585 us (1.12)
  blocking collectives: 132 us -> 257 us
  waiting for transfers between devices: 337 us -> 266 us
  starting transfers between devices: 12.2 us -> 21.5 us
    all_to_all x0 -> x1, blocking collectives: none -> 104 us  [from_root(): lax.all_to_all(jnp.stack([own] * lax.axis_size(axis)), axis, 0, 0)]
    all_gather x1 -> x0, waiting for transfers between devices: 92.5 us -> none  [from_root(): lax.all_gather(own, axis, axis=0, tiled=True)[:len(lines)]]
    all_to_all x2, waiting for transfers between devices: 46.9 us -> 70.3 us  [from_everyone(): lax.all_to_all(jnp.broadcast_to(shard[None], (peers, *shard.shape)), axis...]
    all_to_all x2, blocking collectives: 114 us -> 136 us  [summed_on_arrival(): lax.all_to_all(pieces, axis, split_axis=0, concat_axis=0, tiled=True)]
    all_to_all x2, starting transfers between devices: 12.1 us -> 21.3 us  [from_everyone(): lax.all_to_all(jnp.broadcast_to(shard[None], (peers, *shard.shape)), axis...]
  transfers between devices with their start and end apart: 6 -> 5, of which waited for: 5 -> 5; matrix products, arithmetic and copies ran while one was open for 1% -> 1% of each run, Pallas kernels for 0% -> 0%
where the time goes in v1:
time: 585 us; the launch traced here: 584 us
  waiting for transfers between devices  266 us (45%)
  blocking collectives  257 us (44%)
  starting transfers between devices  21.5 us (4%)
  matrix products  14.1 us (2%)
  between operations  13.9 us (2%)
  local copies, waits for them, and re-layouts  8.39 us (1%)
    all_to_all x2, blocking collectives, summed_on_arrival(): lax.all_to_all(pieces, axis, split_axis=0, concat_axis=0, tiled=True)  136 us
    reduce_scatter x1, waiting for transfers between devices, from_root(): own = lax.psum_scatter(padded, axis, scatter_dimension=0, tiled=True)  126 us
    all_to_all x1, blocking collectives, from_root(): lax.all_to_all(jnp.stack([own] * lax.axis_size(axis)), axis, 0, 0)  104 us
    all_to_all x2, waiting for transfers between devices, from_everyone(): lax.all_to_all(jnp.broadcast_to(shard[None], (peers, *shard.shape)), axis...  70.3 us
    all_gather x2, waiting for transfers between devices, all_blocks(): pieces = lax.all_gather(pieces, axes[k], axis=0, tiled=True)  70 us
    all_to_all x2, starting transfers between devices, from_everyone(): lax.all_to_all(jnp.broadcast_to(shard[None], (peers, *shard.shape)), axis...  21.3 us
    all_gather x1, blocking collectives, all_blocks(): pieces = lax.all_gather(pieces, axes[k], axis=0, tiled=True)  17.8 us
  transfers between devices with their start and end apart: 5, of which 5 were waited for; matrix products, arithmetic and copies ran while one was open for 1% of the time, Pallas kernels for 0%

profile of v1, /device:TPU:1, one launch (start us, length us, event | category | flops | bytes accessed | tf_op | source)
XLA Modules:
  0.0 584.3 jit_solution(5744831641349422391)
XLA Ops:
  7.2 0.0 all-gather.4.cloned.1.call-start
  7.2 17.8 %all-gather = bf16[256,1024]{1,0:T(8,128)(2,1)} all-gather(bf16[64,1024]{1,0:T(8,128)(2,1)} %param.2), channel_id=2, replica_groups=mesh['row_0'=4,'row_1'=4,'row_2'=2,'col'=16] {'row_0'}, dimensions={0}, use_global_device_ids=true | all-gather | bytes 655360 | tf_op jit(solution)/shard_map/all_gather | solution.py:22
  25.1 0.0 all-gather.4.cloned.1.call-update
  25.1 0.0 all-gather.6.cloned.1.call-start
  25.1 42.3 %all-gather.4.cloned.1.call-done = bf16[16,64,1024]{2,1,0:T(8,128)(2,1)} async-done(((bf16[4,64,1024]{2,1,0:T(8,128)(2,1)}), bf16[16,64,1024]{2,1,0:T(8,128)(2,1)}) %all-gather.4.cloned.1.call-update) | async-done | bytes 2097168 | tf_op jit(solution)/shard_map/all_gather | solution.py:22
  67.4 0.0 all-gather.6.cloned.1.call-update
  67.5 0.0 reduce-scatter.2.cloned.1.call-start
  67.5 27.7 %all-gather.6.cloned.1.call-done = bf16[32,64,1024]{2,1,0:T(8,128)(2,1)} async-done(((bf16[16,64,1024]{2,1,0:T(8,128)(2,1)}), bf16[32,64,1024]{2,1,0:T(8,128)(2,1)}) %all-gather.6.cloned.1.call-update) | async-done | bytes 4194320 | tf_op jit(solution)/shard_map/all_gather | solution.py:22
  95.3 2.6 copy.6
  97.9 0.0 copy-start
  97.9 1.9 copy-done
  99.8 1.9 dynamic-slice_select_fusion
  101.7 0.0 reduce-scatter.2.cloned.1.call-update
  101.7 125.9 %reduce-scatter.2.cloned.1.call-done = bf16[128,512]{1,0:T(8,128)(2,1)} async-done(((bf16[2048,512]{1,0:T(8,128)(2,1)}), bf16[128,512]{1,0:T(8,128)(2,1)}) %reduce-scatter.2.cloned.1.call-update) | async-done | bytes 131088 | tf_op jit(solution)/shard_map/reduce_scatter | solution.py:45
  227.6 1.1 stack.2
  228.7 0.0 copy-start.2
  228.7 103.7 %all_to_all.25 = bf16[16,128,512]{2,1,0:T(8,128)(2,1)} all-to-all(bf16[16,128,512]{2,1,0:T(8,128)(2,1)S(1)} %stack.2), channel_id=1, replica_groups=mesh['row_0'=4,'row_1'=4,'row_2'=2,'col'=16] {'col'}, dimensions={0} | all-to-all | bytes 4194304 | tf_op jit(solution)/shard_map/all_to_all | solution.py:47
  332.4 0.0 copy-done.2
  332.4 1.6 broadcast_in_dim.10
  334.0 9.4 %all-to-all-start.1 = ((f32[32,1024,16]{1,2,0:T(8,128)}), f32[32,1024,16]{1,2,0:T(8,128)}, u32[]{:S(2)}, u32[]{:S(2)}) async-start(f32[32,1024,16]{1,2,0:T(8,128)} %broadcast_in_dim.10), calls=%async_computation.2 | async-start | bytes 4194304 | tf_op jit(solution)/shard_map/all_to_all | solution.py:53
  343.5 5.2 convolution_multiply_fusion
  348.7 0.0 copy-start.1
  348.7 43.0 %all-to-all-done.1 = f32[32,1024,16]{1,2,0:T(8,128)} async-done(((f32[32,1024,16]{1,2,0:T(8,128)}), f32[32,1024,16]{1,2,0:T(8,128)}, u32[]{:S(2)}, u32[]{:S(2)}) %all-to-all-start.1) | async-done | bytes 2097184 | tf_op jit(solution)/shard_map/all_to_all | solution.py:53
  391.7 5.4 convolution_add_fusion
  397.1 50.9 %all_to_all.26 = f32[16,512,32]{1,2,0:T(8,128)S(1)} all-to-all(f32[16,512,32]{1,2,0:T(8,128)S(1)} %bitcast.30), channel_id=1, replica_groups=mesh['row_0'=4,'row_1'=4,'row_2'=2,'col'=16] {'col'}, dimensions={0} | all-to-all | bytes 2097152 | tf_op jit(solution)/shard_map/all_to_all | solution.py:70
  448.0 0.1 reduce_sum.18
  448.0 0.0 copy-start.3
  448.0 1.1 broadcast_in_dim.22
  449.1 11.9 %all-to-all-start.3 = ((f32[16,512,32]{1,2,0:T(8,128)}), f32[16,512,32]{1,2,0:T(8,128)S(1)}, u32[]{:S(2)}, u32[]{:S(2)}) async-start(f32[16,512,32]{1,2,0:T(8,128)} %broadcast_in_dim.22), calls=%async_computation.4 | async-start | bytes 2097152 | tf_op jit(solution)/shard_map/all_to_all | solution.py:53
  461.0 27.3 %all-to-all-done.3 = f32[16,512,32]{1,2,0:T(8,128)S(1)} async-done(((f32[16,512,32]{1,2,0:T(8,128)}), f32[16,512,32]{1,2,0:T(8,128)S(1)}, u32[]{:S(2)}, u32[]{:S(2)}) %all-to-all-start.3) | async-done | bytes 1048608 | tf_op jit(solution)/shard_map/all_to_all | solution.py:53
  488.4 0.0 copy-done.1
  488.4 3.5 convolution_multiply_fusion.1
  491.9 0.0 copy-done.3
  491.9 0.3 add_dynamic-update-slice_fusion
  492.3 84.7 %all_to_all.27 = f32[32,1024,16]{1,2,0:T(8,128)S(1)} all-to-all(f32[32,1024,16]{1,2,0:T(8,128)S(1)} %bitcast.24), channel_id=1, replica_groups=mesh['row_0'=4,'row_1'=4,'row_2'=2,'col'=16] {'row_0','row_1','row_2'}, dimensions={0} | all-to-all | bytes 4194304 | tf_op jit(solution)/shard_map/all_to_all | solution.py:70
  577.0 0.1 reduce_sum.19
  577.1 0.6 multiply_add_fusion
Async XLA Ops:
  7.2 60.3 %all-gather.4.cloned.1.call-start = ((), (), s32[]{:S(2)}) async-start(), calls=%async_computation.6 | async-start | bytes 2621440 | tf_op jit(solution)/shard_map/all_gather | solution.py:22
  25.1 70.2 %all-gather.6.cloned.1.call-start = ((), (), s32[]{:S(2)}) async-start(), calls=%async_computation.7 | async-start | bytes 6291456 | tf_op jit(solution)/shard_map/all_gather | solution.py:22
  67.5 160.1 %reduce-scatter.2.cloned.1.call-start = ((), (), s32[]{:S(2)}) async-start(), calls=%async_computation.8 | async-start | bytes 2228224 | tf_op jit(solution)/shard_map/reduce_scatter | solution.py:45
  97.9 1.9 copy-start
  228.7 103.7 %copy-start.2 = (f32[1024,16]{0,1:T(8,128)S(1)}, f32[1024,16]{0,1:T(8,128)}, u32[]{:S(2)}) copy-start(f32[1024,16]{0,1:T(8,128)} %param.3) | copy-start | bytes 196612
  334.0 57.6 %all-to-all-start.1 = ((f32[32,1024,16]{1,2,0:T(8,128)}), f32[32,1024,16]{1,2,0:T(8,128)}, u32[]{:S(2)}, u32[]{:S(2)}) async-start(f32[32,1024,16]{1,2,0:T(8,128)} %broadcast_in_dim.10), calls=%async_computation.2 | async-start | bytes 4194304 | tf_op jit(solution)/shard_map/all_to_all | solution.py:53
  348.7 139.7 %copy-start.1 = (f32[512,1024]{1,0:T(8,128)}, f32[512,1024]{1,0:T(8,128)S(1)}, u32[]{:S(2)}) copy-start(f32[512,1024]{1,0:T(8,128)S(1)} %convolution_multiply_fusion) | copy-start | bytes 6291460
  448.0 43.9 %copy-start.3 = (f32[512,32]{0,1:T(8,128)}, f32[512,32]{0,1:T(8,128)S(1)}, u32[]{:S(2)}) copy-start(f32[512,32]{0,1:T(8,128)S(1)} %reduce_sum.18) | copy-start | bytes 196612
  449.1 39.2 %all-to-all-start.3 = ((f32[16,512,32]{1,2,0:T(8,128)}), f32[16,512,32]{1,2,0:T(8,128)S(1)}, u32[]{:S(2)}, u32[]{:S(2)}) async-start(f32[16,512,32]{1,2,0:T(8,128)} %broadcast_in_dim.22), calls=%async_computation.4 | async-start | bytes 2097152 | tf_op jit(solution)/shard_map/all_to_all | solution.py:53
Sparse Core Ops, SparseCore 0:
  25.2 42.1 all-gather.3
  69.5 25.6 all-gather.5
  101.8 125.7 reduce-scatter.1
